TPU v7x, 32 devices: a whole 2x2x4 slice. The times are simulated.
32 devices in a mesh: segment: 2 (over core), expert: 16 (over z, y, x).
Axes of the slice: x: 2, y: 2, z: 4, core: 2. Of those that a mesh axis runs over, the one named last changes fastest.
Arguments:
- tokens: bfloat16 [2, 1024, 2048], P(None, 'expert'), may hold values from -6 to 6
- routing: int32 [2, 2, 1024, 8], P(None, None, 'expert'), may hold values from 0 to 15, all different within a row; in each aligned block of 64 rows (0 to 63, 64 to 127, ..., all dimensions but the last counted through in order) at most 64 rows name the same one
- norm_gain: bfloat16 [2, 2048], P('segment'), may hold values from 0.5 to 1.5
- router_weight: bfloat16 [2, 2048, 16], P('segment'), may hold values from -0.125 to 0.125
- expert_gate_up: bfloat16 [2, 16, 2048, 768], P('segment', 'expert'), may hold values from -0.125 to 0.125
- expert_down: bfloat16 [2, 16, 384, 2048], P('segment', 'expert'), may hold values from -0.3125 to 0.3125
- pair_index: int32 [64], replicated, may hold values from 0 to 63, each once
- topic_ids: int32 [64], replicated, may hold values from 0 to 7
Outputs:
- final_hidden: bfloat16 [2, 1024, 2048], P('segment', 'expert')
- query_loss: float32 [64], P(('segment', 'expert'))
Inputs may be any that keep to these rules, and one draw needn't show every extreme that they name: `routing`: each row names 8 different experts. In the rows of one device (each aligned block of 64 token rows of one layer and micro-batch) no expert is named by more than 64 rows, a bound that some block reaches. `pair_index`: every passage is the positive of exactly one query.
All inputs are finite; a program needn't handle non-finite values.
Results may differ from a plain program's by a relative error of at most 0.0059.
Values may be sent and summed in bfloat16 or wider, within the bound.
A program may use at most 128 MiB of HBM per device.

v0:
```python
import jax
import jax.numpy as jnp
from jax import lax
from jax.sharding import PartitionSpec as P

SEQ = 16


EPSILON = 1e-06
SOFTMAX_WARMTH = 0.05


def passed_along(block, axis, distance):
    devices = range(lax.axis_size(axis))
    route = [(i - distance, i) for i in devices if i - distance in devices]
    return lax.ppermute(block, axis, route)


def expert_block(received, gate_up, down_proj):
    source_count, slot_count, model_width = received.shape
    flat_rows = received.reshape(source_count * slot_count, model_width)
    projected = jnp.dot(flat_rows, gate_up, preferred_element_type=jnp.float32)
    half_width = gate_up.shape[1] // 2
    hidden = (jax.nn.silu(projected[:, :half_width]) * projected[:, half_width:]).astype(
        jnp.bfloat16
    )
    result = jnp.dot(hidden, down_proj, preferred_element_type=jnp.float32).astype(jnp.bfloat16)
    return result.reshape(source_count, slot_count, model_width)


def moe_layer(inputs, routes, norm_gain, router_weight, gate_up, down_proj):
    row_count, model_width = inputs.shape
    top_count = routes.shape[1]
    expert_count = router_weight.shape[1]
    capacity = 2 * row_count * top_count // expert_count
    widened = inputs.astype(jnp.float32)
    normed = (
        widened
        * lax.rsqrt(jnp.mean(widened * widened, axis=1, keepdims=True) + EPSILON)
        * norm_gain.astype(jnp.float32)
    ).astype(jnp.bfloat16)
    similarity_logits = jnp.dot(normed, router_weight, preferred_element_type=jnp.float32)
    chosen = jnp.take_along_axis(similarity_logits, routes, axis=1)
    raised = jnp.exp(chosen)
    gate_weights = raised / jnp.sum(raised, axis=1, keepdims=True)
    flat_ids = routes.reshape(-1)
    one_hot = (flat_ids[:, None] == jnp.arange(expert_count, dtype=jnp.int32)[None, :]).astype(
        jnp.int32
    )
    earlier = jnp.cumsum(one_hot, axis=0) - one_hot
    slot_index = jnp.sum(earlier * one_hot, axis=1)
    target = flat_ids * capacity + slot_index
    repeated = jnp.repeat(normed, top_count, axis=0)
    outgoing = (
        jnp.zeros((expert_count * capacity, model_width), jnp.bfloat16).at[target].set(repeated)
    )
    outgoing = outgoing.reshape(expert_count, capacity, model_width)
    answered = expert_block(
        lax.all_to_all(outgoing, "expert", split_axis=0, concat_axis=0, tiled=True),
        gate_up,
        down_proj,
    )
    returned = lax.all_to_all(answered, "expert", split_axis=0, concat_axis=0, tiled=True)
    picked = returned.reshape(expert_count * capacity, model_width)[target].astype(jnp.float32)
    picked = picked.reshape(row_count, top_count, model_width)
    mixture = jnp.sum(picked * gate_weights[:, :, None], axis=1)
    return (widened + mixture).astype(jnp.bfloat16)


def pooled_embeddings(final_rows):
    widened = final_rows.astype(jnp.float32)
    pooled = jnp.mean(widened.reshape(-1, SEQ, widened.shape[1]), axis=1)
    return (pooled * lax.rsqrt(jnp.sum(pooled * pooled, axis=1, keepdims=True) + EPSILON)).astype(
        jnp.bfloat16
    )


def local(
    tokens, routing, norm_gain, router_weight, expert_gate_up, expert_down, pair_index, topic_ids
):
    segment_index = lax.axis_index("segment")
    micro_count = tokens.shape[0]
    segment_routes = lax.dynamic_index_in_dim(routing, segment_index, 0, keepdims=False)
    carried = jnp.zeros_like(tokens[0])
    finished = []
    for time_step in range(micro_count + 1):
        fresh_rows = tokens[min(time_step, micro_count - 1)]
        segment_input = jnp.where(segment_index == 0, fresh_rows, carried)
        micro_pick = jnp.clip(time_step - segment_index, 0, micro_count - 1)
        layer_routes = lax.dynamic_index_in_dim(segment_routes, micro_pick, 0, keepdims=False)
        produced = moe_layer(
            segment_input,
            layer_routes,
            norm_gain[0],
            router_weight[0],
            expert_gate_up[0, 0],
            expert_down[0, 0],
        )
        finished.append(produced)
        if time_step < micro_count:
            carried = passed_along(produced, "segment", 1)
    sent_back = passed_along(finished[1], "segment", -1)
    final_rows = jnp.where(segment_index == 0, sent_back, finished[micro_count])
    embedded = pooled_embeddings(final_rows)
    half_count = embedded.shape[0] // 2
    query_vectors = embedded[:half_count]
    passage_vectors = embedded[half_count:]
    device_flat = lax.axis_index(("segment", "expert"))
    columns = jnp.arange(topic_ids.shape[0], dtype=jnp.int32)
    matched = pair_index[:, None] == columns[None, :]
    positive_topic = jnp.sum(
        jnp.where(matched, topic_ids[None, :], jnp.zeros_like(topic_ids)[None, :]), axis=1
    )
    every_query_row = lax.all_gather(query_vectors, ("segment", "expert"), axis=0, tiled=True)
    local_ids = device_flat * half_count + jnp.arange(half_count, dtype=jnp.int32)
    local_topics = lax.dynamic_slice_in_dim(topic_ids, device_flat * half_count, half_count)
    pair_scores = (
        jnp.dot(every_query_row, passage_vectors.T, preferred_element_type=jnp.float32)
        / SOFTMAX_WARMTH
    )
    is_positive = pair_index[:, None] == local_ids[None, :]
    kept_pairs = is_positive | (local_topics[None, :] != positive_topic[:, None])
    partition_part = jnp.sum(
        jnp.where(kept_pairs, jnp.exp(pair_scores), jnp.zeros_like(pair_scores)), axis=1
    )
    positive_part = jnp.sum(
        jnp.where(is_positive, pair_scores, jnp.zeros_like(pair_scores)), axis=1
    )
    partition, positive = (
        lax.psum_scatter(partition_part, ("segment", "expert"), scatter_dimension=0, tiled=True),
        lax.psum_scatter(positive_part, ("segment", "expert"), scatter_dimension=0, tiled=True),
    )
    query_loss = jnp.log(partition) - positive
    return (final_rows[None], query_loss)


def solution(mesh):
    in_specs = (
        P(None, "expert", None),
        P(None, None, "expert", None),
        P("segment", None),
        P("segment", None, None),
        P("segment", "expert", None, None),
        P("segment", "expert", None, None),
        P(),
        P(),
    )
    out_specs = (P("segment", "expert", None), P(("segment", "expert")))
    return jax.shard_map(local, mesh=mesh, in_specs=in_specs, out_specs=out_specs, check_vma=False)
```

profile of v0, /device:TPU:1, one launch (start us, length us, event | category | flops | bytes accessed | tf_op | source)
XLA Modules:
  0.0 793.0 jit_solution(5908741902070264360)
XLA Ops:
  6.5 6.2 scatter_custom_fusion
  12.6 99.4 %all_to_all.30 = bf16[16,64,2048]{2,1,0:T(8,128)(2,1)S(1)} all-to-all(bf16[16,64,2048]{2,1,0:T(8,128)(2,1)} %bitcast.211), channel_id=1, replica_groups=mesh['segment'=2,'expert'=16] {'expert'}, dimensions={0} | all-to-all | bytes 8388608 | tf_op jit(solution)/shard_map/all_to_all | solution.py:59
  112.0 3.4 fusion.7
  115.4 4.3 convolution_convert_fusion.2
  119.8 5.6 all-to-all-start.1
  127.1 3.9 gather_fusion.3
  132.7 70.7 %all-to-all-done.1 = bf16[16,64,2048]{2,1,0:T(8,128)(2,1)} async-done(((bf16[16,64,2048]{2,1,0:T(8,128)(2,1)}), bf16[16,64,2048]{2,1,0:T(8,128)(2,1)}, u32[]{:S(2)}, u32[]{:S(2)}) %all-to-all-start.1) | async-done | bytes 4194336 | tf_op jit(solution)/shard_map/all_to_all | solution.py:63
  203.4 8.0 %gather_fusion = bf16[512,2048]{1,0:T(8,128)(2,1)} fusion(bf16[1024,2048]{1,0:T(8,128)(2,1)} %bitcast.12, s32[1024]{0:T(1024)S(1)} %pad_clamp_fusion.2), kind=kCustom, calls=%fused_computation.3 | custom fusion | bytes 4196352 | tf_op jit(solution)/shard_map/gather | solution.py:64
  211.4 3.4 fusion.2
  218.2 3.5 collective-permute-done
  223.7 6.2 scatter_custom_fusion.1
  229.9 110.4 %all_to_all.31 = bf16[16,64,2048]{2,1,0:T(8,128)(2,1)S(1)} all-to-all(bf16[16,64,2048]{2,1,0:T(8,128)(2,1)} %bitcast.213), channel_id=1, replica_groups=mesh['segment'=2,'expert'=16] {'expert'}, dimensions={0} | all-to-all | bytes 8388608 | tf_op jit(solution)/shard_map/all_to_all | solution.py:59
  340.3 3.4 fusion.5
  343.7 4.3 convolution_convert_fusion.1
  348.0 4.9 all-to-all-start.3
  356.6 3.9 gather_fusion.4
  361.4 69.4 %all-to-all-done.3 = bf16[16,64,2048]{2,1,0:T(8,128)(2,1)} async-done(((bf16[16,64,2048]{2,1,0:T(8,128)(2,1)}), bf16[16,64,2048]{2,1,0:T(8,128)(2,1)}, u32[]{:S(2)}, u32[]{:S(2)}) %all-to-all-start.3) | async-done | bytes 4194336 | tf_op jit(solution)/shard_map/all_to_all | solution.py:63
  430.8 8.0 %gather_fusion.1 = bf16[512,2048]{1,0:T(8,128)(2,1)} fusion(bf16[1024,2048]{1,0:T(8,128)(2,1)} %bitcast.25, s32[1024]{0:T(1024)S(1)} %pad_clamp_fusion.1), kind=kCustom, calls=%fused_computation.4 | custom fusion | bytes 4196352 | tf_op jit(solution)/shard_map/gather | solution.py:64
  438.9 3.4 fusion.1
  444.9 3.5 collective-permute-done.2
  450.5 6.6 scatter_custom_fusion.2
  457.1 110.7 %all_to_all.32 = bf16[16,64,2048]{2,1,0:T(8,128)(2,1)S(1)} all-to-all(bf16[16,64,2048]{2,1,0:T(8,128)(2,1)} %bitcast.212), channel_id=1, replica_groups=mesh['segment'=2,'expert'=16] {'expert'}, dimensions={0} | all-to-all | bytes 8388608 | tf_op jit(solution)/shard_map/all_to_all | solution.py:59
  567.8 3.4 fusion.3
  571.2 4.3 convolution_convert_fusion
  575.6 4.9 all-to-all-start.5
  581.0 4.8 collective-permute-start.1
  586.9 3.9 gather_fusion.5
  591.1 67.0 %all-to-all-done.5 = bf16[16,64,2048]{2,1,0:T(8,128)(2,1)} async-done(((bf16[16,64,2048]{2,1,0:T(8,128)(2,1)}), bf16[16,64,2048]{2,1,0:T(8,128)(2,1)}, u32[]{:S(2)}, u32[]{:S(2)}) %all-to-all-start.5) | async-done | bytes 4194336 | tf_op jit(solution)/shard_map/all_to_all | solution.py:63
  658.2 8.0 %gather_fusion.2 = bf16[512,2048]{1,0:T(8,128)(2,1)} fusion(bf16[1024,2048]{1,0:T(8,128)(2,1)} %bitcast.36, s32[1024]{0:T(1024)S(1)} %pad_clamp_fusion), kind=kCustom, calls=%fused_computation.5 | custom fusion | bytes 4196352 | tf_op jit(solution)/shard_map/gather | solution.py:64
  666.1 3.4 fusion
  670.7 85.3 %all-gather = bf16[32,2,2048]{2,1,0:T(2,128)(2,1)S(1)} all-gather(bf16[1,2,2048]{2,1,0:T(2,128)(2,1)S(1)} %slice_bitcast_fusion), channel_id=1, replica_groups=mesh['segment'=2,'expert'=16] {'segment','expert'}, dimensions={0}, use_global_device_ids=true | all-gather | bytes 270336 | tf_op jit(solution)/shard_map/all_gather | solution.py:114
  758.0 34.0 %all-reduce.2 = (f32[64]{0:T(128)S(1)}, f32[64]{0:T(128)S(1)}) all-reduce(f32[64]{0:T(128)S(1)} %get-tuple-element.4, f32[64]{0:T(128)S(1)} %get-tuple-element.3), channel_id=3, replica_groups=mesh['segment'=2,'expert'=16] {'segment','expert'}, use_global_device_ids=true, to_apply=%region_27.29.clone | all-reduce | flops 128 | bytes 1024
  (113 shorter events, 29.0 us)
Async XLA Ops:
  0.6 111.4 %copy-start = (bf16[1,1,2048,768]{3,2,1,0:T(8,128)(2,1)S(1)}, bf16[1,1,2048,768]{3,2,1,0:T(8,128)(2,1)}, u32[]{:S(2)}) copy-start(bf16[1,1,2048,768]{3,2,1,0:T(8,128)(2,1)} %param.14) | copy-start | bytes 9437188
  112.0 3.4 copy-start.5
  119.8 6.1 copy-start.3
  119.8 83.6 %all-to-all-start.1 = ((bf16[16,64,2048]{2,1,0:T(8,128)(2,1)}), bf16[16,64,2048]{2,1,0:T(8,128)(2,1)}, u32[]{:S(2)}, u32[]{:S(2)}) async-start(bf16[16,64,2048]{2,1,0:T(8,128)(2,1)} %bitcast.215), calls=%async_computation.1 | async-start | bytes 8388608 | tf_op jit(solution)/shard_map/all_to_all | solution.py:63
  216.6 5.1 collective-permute-start
  222.9 0.7 copy-start.1
  340.2 3.4 copy-start.6
  348.0 82.8 %all-to-all-start.3 = ((bf16[16,64,2048]{2,1,0:T(8,128)(2,1)}), bf16[16,64,2048]{2,1,0:T(8,128)(2,1)}, u32[]{:S(2)}, u32[]{:S(2)}) async-start(bf16[16,64,2048]{2,1,0:T(8,128)(2,1)} %bitcast.216), calls=%async_computation.3 | async-start | bytes 8388608 | tf_op jit(solution)/shard_map/all_to_all | solution.py:63
  356.4 4.1 copy-start.4
  430.8 11.5 %copy-start.2 = (bf16[64,2048]{1,0:T(8,128)(2,1)S(1)}, bf16[64,2048]{1,0:T(8,128)(2,1)}, u32[]{:S(2)}) copy-start(bf16[64,2048]{1,0:T(8,128)(2,1)} %copy-done.1) | copy-start | bytes 786436
  438.9 5.7 slice-start
  443.1 5.3 collective-permute-start.2
  567.8 3.4 copy-start.7
  575.6 5.1 copy-start.8
  575.6 5.2 copy-start.9
  575.6 82.6 %all-to-all-start.5 = ((bf16[16,64,2048]{2,1,0:T(8,128)(2,1)}), bf16[16,64,2048]{2,1,0:T(8,128)(2,1)}, u32[]{:S(2)}, u32[]{:S(2)}) async-start(bf16[16,64,2048]{2,1,0:T(8,128)(2,1)} %bitcast.214), calls=%async_computation.5 | async-start | bytes 8388608 | tf_op jit(solution)/shard_map/all_to_all | solution.py:63
  581.0 88.6 %collective-permute-start.1 = (bf16[64,2048]{1,0:T(8,128)(2,1)}, bf16[64,2048]{1,0:T(8,128)(2,1)}, u32[]{:S(2)}, u32[]{:S(2)}) collective-permute-start(bf16[64,2048]{1,0:T(8,128)(2,1)} %fusion.45), channel_id=1, source_target_pairs={{16,0},{17,1},{18,2},{19,3},{20,4},{21,5},{22,6},{23,7},{24,8},{25... | collective-permute-start | bytes 786440 | tf_op jit(solution)/shard_map/ppermute | solution.py:16
where the time goes:
time: 804 us; the launch traced here: 793 us
  blocking collectives  440 us (55%)
  waiting for transfers between devices  214 us (27%)
  local copies, waits for them, and re-layouts  60.1 us (7%)
  other arithmetic  27.5 us (3%)
  matrix products  26.9 us (3%)
  starting transfers between devices  23 us (3%)
    all_to_all x3, blocking collectives, moe_layer(): lax.all_to_all(outgoing, 'expert', split_axis=0, concat_axis=0, tiled=True)  320 us
    all_to_all x3, waiting for transfers between devices, moe_layer(): lax.all_to_all(answered, 'expert', split_axis=0, concat_axis=0, tiled=True)  207 us
    all_gather x1, blocking collectives, local(): lax.all_gather(query_vectors, ('segment', 'expert'), axis=0, tiled=True)  85.3 us
    unnamed x1, blocking collectives  34 us
    gather x3, local copies, waits for them, and re-layouts, moe_layer(): returned.reshape(expert_count * capacity, model_width)[target]  24 us
    scatter x3, local copies, waits for them, and re-layouts, moe_layer(): jnp.zeros((expert_count * capacity, model_width), jnp.bfloat16).at[target]  18.9 us
  transfers between devices with their start and end apart: 6, of which 5 were waited for; matrix products, arithmetic and copies ran while one was open for 4% of the time, Pallas kernels for 0%

commit v1 on v0

v1 whole, which is shorter than its diff:
```python
import jax
import jax.numpy as jnp
from jax import lax
from jax.sharding import PartitionSpec as P

SEQ = 16


EPSILON = 1e-06
SOFTMAX_WARMTH = 0.05


def pooled_embeddings(final_rows):
    widened = final_rows.astype(jnp.float32)
    pooled = jnp.mean(widened.reshape(-1, SEQ, widened.shape[1]), axis=1)
    return (pooled * lax.rsqrt(jnp.sum(pooled * pooled, axis=1, keepdims=True) + EPSILON)).astype(
        jnp.bfloat16
    )


def normalised(rows, gain):
    widened = rows.astype(jnp.float32)
    return (
        widened
        * lax.rsqrt(jnp.mean(widened * widened, axis=1, keepdims=True) + EPSILON)
        * gain.astype(jnp.float32)
    ).astype(jnp.bfloat16)


def dense_gates(normed, routes, router_weight):
    expert_count = router_weight.shape[1]
    logits = jnp.dot(normed, router_weight, preferred_element_type=jnp.float32)
    experts = jnp.arange(expert_count, dtype=jnp.int32)
    named = jnp.any(routes[:, :, None] == experts[None, None, :], axis=1)
    raised = jnp.where(named, jnp.exp(logits), 0.0)
    return raised / jnp.sum(raised, axis=1, keepdims=True)


def contrastive(final_rows, pair_index, topic_ids):
    embedded = pooled_embeddings(final_rows)
    half_count = embedded.shape[0] // 2
    own_queries = embedded[:half_count]
    passages = lax.all_gather(embedded[half_count:], ("segment", "expert"), axis=0, tiled=True)
    device_flat = lax.axis_index(("segment", "expert"))
    positive = lax.dynamic_slice_in_dim(pair_index, device_flat * half_count, half_count)
    columns = jnp.arange(topic_ids.shape[0], dtype=jnp.int32)
    is_positive = positive[:, None] == columns[None, :]
    positive_topic = jnp.sum(jnp.where(is_positive, topic_ids[None, :], 0), axis=1)
    kept = is_positive | (topic_ids[None, :] != positive_topic[:, None])
    scores = (
        jnp.dot(own_queries, passages.T, preferred_element_type=jnp.float32) / SOFTMAX_WARMTH
    )
    partition = jnp.sum(jnp.where(kept, jnp.exp(scores), 0.0), axis=1)
    return jnp.log(partition) - jnp.sum(jnp.where(is_positive, scores, 0.0), axis=1)


def gathered(
    tokens, routing, norm_gain, router_weight, expert_gate_up, expert_down, pair_index, topic_ids
):
    segment_index = lax.axis_index("segment")
    expert_index = lax.axis_index("expert")
    gains = lax.all_gather(norm_gain, "segment", axis=0, tiled=True)
    routers = lax.all_gather(router_weight, "segment", axis=0, tiled=True)

    def by_layer(own):
        other = lax.ppermute(own, "segment", [(0, 1), (1, 0)])
        first = segment_index == 0
        return jnp.where(first, own, other), jnp.where(first, other, own)

    gate_ups = by_layer(expert_gate_up[0, 0])
    downs = by_layer(expert_down[0, 0])
    rows = lax.dynamic_index_in_dim(tokens, segment_index, 0, keepdims=False)
    micro_routes = lax.dynamic_index_in_dim(routing, segment_index, 1, keepdims=False)
    half_width = expert_down.shape[2]
    for layer in range(routing.shape[0]):
        normed = normalised(rows, gains[layer])
        gates = dense_gates(normed, micro_routes[layer], routers[layer])
        own_gate = lax.all_to_all(gates, "expert", split_axis=1, concat_axis=0, tiled=True)
        everyone = lax.all_gather(normed, "expert", axis=0, tiled=True)
        projected = jnp.dot(everyone, gate_ups[layer], preferred_element_type=jnp.float32)
        hidden = (
            jax.nn.silu(projected[:, :half_width]) * projected[:, half_width:]
        ).astype(jnp.bfloat16)
        answer = jnp.dot(hidden, downs[layer], preferred_element_type=jnp.float32)
        part = (answer * own_gate).astype(jnp.bfloat16)
        mixture = lax.psum_scatter(part, "expert", scatter_dimension=0, tiled=True)
        rows = (rows.astype(jnp.float32) + mixture.astype(jnp.float32)).astype(jnp.bfloat16)
    return rows[None], contrastive(rows, pair_index, topic_ids)


def solution(mesh):
    in_specs = (
        P(None, "expert", None),
        P(None, None, "expert", None),
        P("segment", None),
        P("segment", None, None),
        P("segment", "expert", None, None),
        P("segment", "expert", None, None),
        P(),
        P(),
    )
    out_specs = (P("segment", "expert", None), P(("segment", "expert")))
    return jax.shard_map(gathered, mesh=mesh, in_specs=in_specs, out_specs=out_specs, check_vma=False)
```

time: 804 us -> 460 us (0.57); the launches traced: 793 us -> 460 us
  blocking collectives: 440 us -> 89.6 us
  waiting for transfers between devices: 214 us -> 313 us
  local copies, waits for them, and re-layouts: 60.1 us -> 1.72 us
  other arithmetic: 27.5 us -> 8.23 us
  starting transfers between devices: 23 us -> 8.46 us
  between operations: 1.53 us -> 13.9 us
    all_to_all x3 -> x1, blocking collectives: 320 us -> 11.2 us  [gathered(): lax.all_to_all(gates, 'expert', split_axis=1, concat_axis=0, tiled=True)]
    all_to_all x3 -> x1, waiting for transfers between devices: 207 us -> 6.06 us  [gathered(): lax.all_to_all(gates, 'expert', split_axis=1, concat_axis=0, tiled=True)]
    reduce_scatter x0 -> x2, waiting for transfers between devices: none -> 189 us  [gathered(): mixture = lax.psum_scatter(part, 'expert', scatter_dimension=0, tiled=True)]
    all_gather x0 -> x2, waiting for transfers between devices: none -> 117 us  [gathered(): everyone = lax.all_gather(normed, 'expert', axis=0, tiled=True)]
    gather x18 -> x0, local copies, waits for them, and re-layouts: 36.7 us -> none  [the longest x3 24 us: moe_layer(): returned.reshape(expert_count * capacity, model_width)[target]]
    unnamed x1 -> x0, blocking collectives: 34 us -> none
    scatter x3 -> x0, local copies, waits for them, and re-layouts: 18.9 us -> none  [moe_layer(): jnp.zeros((expert_count * capacity, model_width), jnp.bfloat16).at[target]]
    reduce_sum x13 -> x3, other arithmetic: 14.3 us -> 2.43 us  [the longest x2 2.25 us: normalised(): jnp.mean(widened * widened, axis=1, keepdims=True) + EPSILON]
  transfers between devices with their start and end apart: 6 -> 7, of which waited for: 5 -> 5; matrix products, arithmetic and copies ran while one was open for 4% -> 2% of each run, Pallas kernels for 0% -> 0%
where the time goes in v1:
time: 460 us
  waiting for transfers between devices  313 us (68%)
  blocking collectives  89.6 us (19%)
  matrix products  25.3 us (6%)
  between operations  13.9 us (3%)
  starting transfers between devices  8.46 us (2%)
  other arithmetic  8.23 us (2%)
    reduce_scatter x2, waiting for transfers between devices, gathered(): mixture = lax.psum_scatter(part, 'expert', scatter_dimension=0, tiled=True)  189 us
    all_gather x2, waiting for transfers between devices, gathered(): everyone = lax.all_gather(normed, 'expert', axis=0, tiled=True)  117 us
    all_gather x1, blocking collectives, contrastive(): lax.all_gather(embedded[half_count:], ('segment', 'expert'), axis=0, tile...  69.4 us
    dot_general x2, matrix products, gathered(): jnp.dot(everyone, gate_ups[layer], preferred_element_type=jnp.float32)  12.5 us
    all_to_all x1, blocking collectives, gathered(): lax.all_to_all(gates, 'expert', split_axis=1, concat_axis=0, tiled=True)  11.2 us
    dot_general x2, matrix products, gathered(): answer = jnp.dot(hidden, downs[layer], preferred_element_type=jnp.float32)  10.1 us
  transfers between devices with their start and end apart: 7, of which 5 were waited for; matrix products, arithmetic and copies ran while one was open for 2% of the time, Pallas kernels for 0%

profile of v1, /device:TPU:1, one launch (start us, length us, event | category | flops | bytes accessed | tf_op | source)
XLA Modules:
  0.0 459.8 jit_solution(5309216881780363149)
XLA Ops:
  7.2 2.0 all-gather
  9.3 1.1 fusion.21
  10.4 1.8 fusion.23
  12.2 0.3 collective-permute-start
  12.5 0.3 collective-permute-start.1
  12.8 0.7 dynamic-slice_bitcast_fusion.1
  13.5 7.0 %all_gather.17 = bf16[2,2048,16]{1,2,0:T(8,128)(2,1)S(1)} all-gather(bf16[1,2048,16]{1,2,0:T(8,128)(2,1)} %param.11), channel_id=1, replica_groups=mesh['segment'=2,'expert'=16] {'segment'}, dimensions={0}, use_global_device_ids=true | all-gather | bytes 196608 | tf_op jit(solution)/shard_map/all_gather | solution.py:63
  20.5 1.2 fusion.49
  21.7 0.6 broadcast_divide_fusion.1
  22.3 7.7 %all-to-all-start = ((f32[64,16,1]{0,2,1:T(1,128)}), f32[64,16,1]{0,2,1:T(1,128)S(1)}, u32[]{:S(2)}, u32[]{:S(2)}) async-start(f32[64,16,1]{0,2,1:T(1,128)} %bitcast.9), calls=%async_computation | async-start | bytes 16384 | tf_op jit(solution)/shard_map/all_to_all | solution.py:78
  30.1 6.1 %all-to-all-done = f32[64,16,1]{0,2,1:T(1,128)S(1)} async-done(((f32[64,16,1]{0,2,1:T(1,128)}), f32[64,16,1]{0,2,1:T(1,128)S(1)}, u32[]{:S(2)}, u32[]{:S(2)}) %all-to-all-start) | async-done | bytes 4128 | tf_op jit(solution)/shard_map/all_to_all | solution.py:78
  36.3 52.9 %all-gather.5.cloned.1.call-done = bf16[1024,2048]{1,0:T(8,128)(2,1)} async-done(((bf16[64,2048]{1,0:T(8,128)(2,1)}), bf16[1024,2048]{1,0:T(8,128)(2,1)}) %all-gather.5.cloned.1.call-update) | async-done | bytes 4194320 | tf_op jit(solution)/shard_map/all_gather | solution.py:79
  89.2 6.4 %fusion.2 = f32[1024,768]{1,0:T(8,128)S(1)} fusion(bf16[1024,2048]{1,0:T(8,128)(2,1)} %all-gather.5.cloned.1.call-done, bf16[2048,768]{1,0:T(8,128)(2,1)S(1)} %collective-permute-done, pred[]{:T(512)S(6)} %eq.47, bf16[1,1,2048,768]{3,2,1,0:T(8,128)(2,1)} %param.12), kind=kOutput, calls=%fused_computation.4 | convolution fusion | flops 3222798336 | bytes 13631489 | tf_op jit(solution)/shard_map/dot_general | solution.py:80
  95.6 5.7 %multiply_convert_fusion.1 = bf16[1024,2048]{1,0:T(8,128)(2,1)} fusion(f32[1024]{0:T(1024)S(1)} %mul.125, bf16[384,2048]{1,0:T(8,128)(2,1)} %collective-permute-done.1, pred[]{:T(512)S(6)} %eq.47, f32[1024,768]{1,0:T(8,128)S(1)} %fusion.2, bf16[1,1,384,2048]{3,2,1,0:T(8,128)(2,1)S(1)} %copy-done.2), kind=kOutput, calls=%fused_computation.1 | convolution fusion | flops 1617952768 | bytes 10489857 | tf_op jit(solution)/shard_map/dot_general | solution.py:84
  101.5 93.7 %reduce-scatter.3.cloned.1.call-done = bf16[64,2048]{1,0:T(8,128)(2,1)} async-done(((bf16[1024,2048]{1,0:T(8,128)(2,1)}), bf16[64,2048]{1,0:T(8,128)(2,1)}) %reduce-scatter.3.cloned.1.call-update) | async-done | bytes 262160 | tf_op jit(solution)/shard_map/reduce_scatter | solution.py:86
  195.2 1.1 fusion.27
  196.3 0.8 fusion.29
  197.2 1.1 fusion.50
  198.4 11.2 %all_to_all.32 = f32[64,16,1]{0,2,1:T(1,128)S(1)} all-to-all(f32[64,16,1]{0,2,1:T(1,128)S(1)} %bitcast.81), channel_id=1, replica_groups=mesh['segment'=2,'expert'=16] {'expert'}, dimensions={1} | all-to-all | bytes 8192 | tf_op jit(solution)/shard_map/all_to_all | solution.py:78
  209.7 64.1 %all-gather.7.cloned.1.call-done = bf16[1024,2048]{1,0:T(8,128)(2,1)} async-done(((bf16[64,2048]{1,0:T(8,128)(2,1)}), bf16[1024,2048]{1,0:T(8,128)(2,1)}) %all-gather.7.cloned.1.call-update) | async-done | bytes 4194320 | tf_op jit(solution)/shard_map/all_gather | solution.py:79
  273.8 6.1 %fusion = f32[1024,768]{1,0:T(8,128)S(1)} fusion(bf16[1024,2048]{1,0:T(8,128)(2,1)} %all-gather.7.cloned.1.call-done, bf16[2048,768]{1,0:T(8,128)(2,1)} %copy-done.1, pred[]{:T(512)S(6)} %eq.47, bf16[1,1,2048,768]{3,2,1,0:T(8,128)(2,1)} %param.12), kind=kOutput, calls=%fused_computation.2 | convolution fusion | flops 3222798336 | bytes 13631489 | tf_op jit(solution)/shard_map/dot_general | solution.py:80
  280.0 4.3 multiply_convert_fusion
  284.3 0.6 copy-done.4
  285.0 0.2 select_reduce_fusion.1
  285.2 95.7 %reduce-scatter.5.cloned.1.call-done = bf16[64,2048]{1,0:T(8,128)(2,1)} async-done(((bf16[1024,2048]{1,0:T(8,128)(2,1)}), bf16[64,2048]{1,0:T(8,128)(2,1)}) %reduce-scatter.5.cloned.1.call-update) | async-done | bytes 262160 | tf_op jit(solution)/shard_map/reduce_scatter | solution.py:86
  380.9 1.7 convert_reduce_fusion
  382.7 0.1 multiply_reduce_fusion
  382.8 0.1 multiply_convert_fusion.2
  382.9 69.4 %all-gather.1 = bf16[32,2,2048]{2,1,0:T(2,128)(2,1)S(1)} all-gather(bf16[1,2,2048]{2,1,0:T(2,128)(2,1)S(1)} %slice_bitcast_fusion.4), channel_id=1, replica_groups=mesh['segment'=2,'expert'=16] {'segment','expert'}, dimensions={0}, use_global_device_ids=true | all-gather | bytes 270336 | tf_op jit(solution)/shard_map/all_gather | solution.py:43
  452.3 0.1 reshape.77
  452.4 0.3 fusion.39
  452.7 0.5 log_subtract_fusion
  (33 shorter events, 0.6 us)
Async XLA Ops:
  7.2 82.0 %all-gather.5.cloned.1.call-start = ((), (), s32[]{:S(2)}) async-start(), calls=%async_computation.4 | async-start | bytes 4456448 | tf_op jit(solution)/shard_map/all_gather | solution.py:79
  12.2 24.1 %collective-permute-start = (bf16[2048,768]{1,0:T(8,128)(2,1)}, bf16[2048,768]{1,0:T(8,128)(2,1)S(1)}, u32[]{:S(2)}, u32[]{:S(2)}) collective-permute-start(bf16[2048,768]{1,0:T(8,128)(2,1)} %bitcast.83), channel_id=1, source_target_pairs={{0,16},{16,0},{1,17},{17,1},{2,18},{18,2},{3,19},{19,3},{4,20},{20... | collective-permute-start | bytes 9437192 | tf_op jit(solution)/shard_map/ppermute | solution.py:66
  12.5 83.2 %collective-permute-start.1 = (bf16[384,2048]{1,0:T(8,128)(2,1)}, bf16[384,2048]{1,0:T(8,128)(2,1)}, u32[]{:S(2)}, u32[]{:S(2)}) collective-permute-start(bf16[384,2048]{1,0:T(8,128)(2,1)} %bitcast.84), channel_id=1, source_target_pairs={{0,16},{16,0},{1,17},{17,1},{2,18},{18,2},{3,19},{19,3},{4,20},{20... | collective-permute-start | bytes 4718600 | tf_op jit(solution)/shard_map/ppermute | solution.py:66
  22.3 13.9 %all-to-all-start = ((f32[64,16,1]{0,2,1:T(1,128)}), f32[64,16,1]{0,2,1:T(1,128)S(1)}, u32[]{:S(2)}, u32[]{:S(2)}) async-start(f32[64,16,1]{0,2,1:T(1,128)} %bitcast.9), calls=%async_computation | async-start | bytes 16384 | tf_op jit(solution)/shard_map/all_to_all | solution.py:78
  30.1 165.1 %reduce-scatter.3.cloned.1.call-start = ((), (), s32[]{:S(2)}) async-start(), calls=%async_computation.5 | async-start | bytes 4456448 | tf_op jit(solution)/shard_map/reduce_scatter | solution.py:86
  36.3 59.3 %copy-start.1 = (bf16[2048,768]{1,0:T(8,128)(2,1)}, bf16[2048,768]{1,0:T(8,128)(2,1)S(1)}, u32[]{:S(2)}) copy-start(bf16[2048,768]{1,0:T(8,128)(2,1)S(1)} %collective-permute-done) | copy-start | bytes 9437188
  89.2 6.4 %copy-start.2 = (bf16[1,1,384,2048]{3,2,1,0:T(8,128)(2,1)S(1)}, bf16[1,1,384,2048]{3,2,1,0:T(8,128)(2,1)}, u32[]{:S(2)}) copy-start(bf16[1,1,384,2048]{3,2,1,0:T(8,128)(2,1)} %param.13) | copy-start | bytes 4718596
  101.4 93.8 %copy-start = (bf16[2,64,2048]{2,1,0:T(8,128)(2,1)S(1)}, bf16[2,64,2048]{2,1,0:T(8,128)(2,1)}, u32[]{:S(2)}) copy-start(bf16[2,64,2048]{2,1,0:T(8,128)(2,1)} %param.8) | copy-start | bytes 1572868
  101.4 172.4 %all-gather.7.cloned.1.call-start = ((), (), s32[]{:S(2)}) async-start(), calls=%async_computation.6 | async-start | bytes 4456448 | tf_op jit(solution)/shard_map/all_gather | solution.py:79
  197.2 183.8 %reduce-scatter.5.cloned.1.call-start = ((), (), s32[]{:S(2)}) async-start(), calls=%async_computation.7 | async-start | bytes 4456448 | tf_op jit(solution)/shard_map/reduce_scatter | solution.py:86
  209.7 70.2 %copy-start.3 = (bf16[1,1,384,2048]{3,2,1,0:T(8,128)(2,1)S(1)}, bf16[1,1,384,2048]{3,2,1,0:T(8,128)(2,1)}, u32[]{:S(2)}) copy-start(bf16[1,1,384,2048]{3,2,1,0:T(8,128)(2,1)} %param.13) | copy-start | bytes 4718596
  284.3 0.7 copy-start.4
  284.3 0.7 copy-start.5
Sparse Core Ops, SparseCore 0:
  12.3 76.8 all-gather.4
  101.5 93.5 reduce-scatter.2
  198.5 75.2 all-gather.6
  284.5 96.4 reduce-scatter.4

commit v2 on v1

--- a/solution.py
+++ b/solution.py
@@ -1,6 +1,10 @@
+import functools
+
 import jax
 import jax.numpy as jnp
 from jax import lax
+from jax.experimental import pallas as pl
+from jax.experimental.pallas import tpu as pltpu
 from jax.sharding import PartitionSpec as P
 
 SEQ = 16
@@ -36,11 +40,12 @@
     return raised / jnp.sum(raised, axis=1, keepdims=True)
 
 
-def contrastive(final_rows, pair_index, topic_ids):
+def contrastive(final_rows, pair_index, topic_ids, passages=None):
     embedded = pooled_embeddings(final_rows)
     half_count = embedded.shape[0] // 2
     own_queries = embedded[:half_count]
-    passages = lax.all_gather(embedded[half_count:], ("segment", "expert"), axis=0, tiled=True)
+    if passages is None:
+        passages = lax.all_gather(embedded[half_count:], ("segment", "expert"), axis=0, tiled=True)
     device_flat = lax.axis_index(("segment", "expert"))
     positive = lax.dynamic_slice_in_dim(pair_index, device_flat * half_count, half_count)
     columns = jnp.arange(topic_ids.shape[0], dtype=jnp.int32)
@@ -88,6 +93,311 @@
     return rows[None], contrastive(rows, pair_index, topic_ids)
 
 
+LANES = 128
+MESH = pl.DeviceIdType.MESH
+
+
+def sections_kernel(
+    sizes, tokens, routing, guide, gate_up, down, final, passages,
+    rows, guides, ups, downs, spread, parts, first_in, second_in, third_in, embeds,
+    guide_sem, up_sem, down_sem, swap_sem, out_send, out_recv, back_send, back_recv,
+    emb_send, emb_recv, pair_sem,
+):
+    layers, experts, depth, row_count, width = sizes
+    half_rows = row_count // 2
+    half_width = down.shape[2]
+    core, me = lax.axis_index("segment"), lax.axis_index("expert")
+    z, column = me // 4, me % 4
+    y, x = column // 2, column % 2
+    beside_x, beside_y = y * 2 + 1 - x, (1 - y) * 2 + x
+    across = (1 - y) * 2 + 1 - x
+    near, far = (beside_y, beside_x), (beside_x, beside_y)
+
+    barrier = pltpu.get_barrier_semaphore()
+    for step in range(1, experts):
+        pl.semaphore_signal(
+            barrier, inc=1, device_id=(core, (me + step) % experts), device_id_type=MESH
+        )
+    pl.semaphore_signal(barrier, inc=1, device_id=(1 - core, me), device_id_type=MESH)
+    pl.semaphore_wait(barrier, experts)
+
+    def remote(src, dst, sent, received, device):
+        return pltpu.make_async_remote_copy(
+            src_ref=src, dst_ref=dst, send_sem=sent, recv_sem=received,
+            device_id=device, device_id_type=MESH,
+        )
+
+    weights = ((guide, guides, guide_sem), (gate_up.at[0, 0], ups, up_sem),
+               (down.at[0, 0], downs, down_sem))
+    swaps = []
+    for i, (src, dst, sem) in enumerate(weights):
+        pltpu.make_async_copy(src, dst.at[core], sem.at[core]).start()
+        swap = remote(src, dst.at[core], swap_sem.at[i], sem.at[core], (1 - core, me))
+        swap.start()
+        swaps.append(swap)
+
+    rows[...] = tokens[core]
+
+    def landed(i, layer):
+        src, dst, sem = weights[i]
+        pltpu.make_async_copy(src, dst.at[layer], sem.at[layer]).wait()
+
+    def layer_body(layer, carry):
+        landed(0, layer)
+        widened = rows[...].astype(jnp.float32)
+        gain = guides[layer, pl.ds(LANES, 16), :][:1].astype(jnp.float32)
+        normed = (
+            widened
+            * lax.rsqrt(jnp.mean(widened * widened, axis=1, keepdims=True) + EPSILON)
+            * gain
+        ).astype(jnp.bfloat16)
+        logits = lax.dot_general(
+            normed, guides[layer, pl.ds(0, LANES), :], (((1,), (1,)), ((), ())),
+            preferred_element_type=jnp.float32,
+        )
+        lane = lax.broadcasted_iota(jnp.int32, (row_count, LANES), 1)
+        routes = routing[layer, core]
+        named = lane < 0
+        for k in range(routes.shape[1]):
+            named = named | (routes[:, k : k + 1] == lane % experts)
+        raised = jnp.where(named, jnp.exp(logits), 0.0)
+        gates = raised / jnp.sum(jnp.where(lane < experts, raised, 0.0), axis=1, keepdims=True)
+        coarse = gates.astype(jnp.bfloat16).astype(jnp.float32)
+        coded = jnp.where(
+            lane < experts, coarse, jnp.where(lane < 2 * experts, gates - coarse, 0.0)
+        ).astype(jnp.bfloat16)
+        for h in range(2):
+            here = slice(h * half_rows, (h + 1) * half_rows)
+            spread[layer, h, column, z, :, pl.ds(0, width)] = normed[here]
+            spread[layer, h, column, z, :, pl.ds(width, LANES)] = coded[here]
+
+        sends = []
+
+        def pass_on(h, block_column, block_z, device):
+            slot = spread.at[layer, h, block_column, block_z]
+            number = sum(1 for g, _ in sends if g == h)
+            copy = remote(
+                slot, slot, out_send.at[layer, h, number],
+                out_recv.at[layer, h, block_column, block_z], (core, device),
+            )
+            copy.start()
+            sends.append((h, copy))
+
+        def arrived(h, block_column, block_z):
+            slot = spread.at[layer, h, block_column, block_z]
+            remote(
+                slot, slot, out_send.at[layer, h, 0],
+                out_recv.at[layer, h, block_column, block_z], (core, me),
+            ).wait_recv()
+
+        for h in range(2):
+            pass_on(h, column, z, z * 4 + near[h])
+        for step in range(1, depth):
+            for h in range(2):
+                pass_on(h, column, z, (z + step) % depth * 4 + column)
+        for step in range(1, depth):
+            for h in range(2):
+                arrived(h, column, (z + depth - step) % depth)
+                pass_on(h, column, (z + depth - step) % depth, z * 4 + near[h])
+        for step in range(depth):
+            for h in range(2):
+                pass_on(h, column, (z + depth - step) % depth, z * 4 + far[h])
+        landed(1, layer)
+        landed(2, layer)
+
+        def answer(columns):
+            held = [spread[layer, h, columns[h]].reshape(depth * half_rows, -1) for h in range(2)]
+            both = jnp.concatenate([b[:, :width] for b in held], axis=0)
+            codes = jnp.concatenate([b[:, width:] for b in held], axis=0).astype(jnp.float32)
+            mine = lax.broadcasted_iota(jnp.int32, codes.shape, 1) % experts == me
+            gate = jnp.sum(jnp.where(mine, codes, 0.0), axis=1, keepdims=True)
+            projected = jnp.dot(both, ups[layer], preferred_element_type=jnp.float32)
+            lifted = projected[:, :half_width]
+            hidden = (
+                lifted / (1.0 + jnp.exp(-lifted)) * projected[:, half_width:]
+            ).astype(jnp.bfloat16)
+            result = jnp.dot(hidden, downs[layer], preferred_element_type=jnp.float32)
+            part = (result * gate).astype(jnp.bfloat16)
+            part = part.reshape(2, depth, half_rows, width)
+            for h in range(2):
+                parts[layer, h, columns[h]] = part[h]
+
+        backs = []
+
+        def send_back(h, src, dst, received, device):
+            number = sum(1 for g, _ in backs if g == h)
+            copy = remote(
+                src, dst, back_send.at[layer, h, number], back_recv.at[layer, h, received],
+                (core, device),
+            )
+            copy.start()
+            backs.append((h, copy))
+
+        def came_back(h, dst, received):
+            remote(
+                dst, dst, back_send.at[layer, h, 0], back_recv.at[layer, h, received], (core, me)
+            ).wait_recv()
+
+        answer((column, column))
+        for step in range(depth):
+            for h in range(2):
+                block = (z + depth - step) % depth
+                arrived(h, near[h], block)
+                pass_on(h, near[h], block, z * 4 + far[h])
+        answer(near)
+        for step in range(depth):
+            for h in range(2):
+                block = (z + step) % depth
+                send_back(
+                    h, parts.at[layer, h, near[h], block], first_in.at[layer, h, 0, block],
+                    block, z * 4 + near[h],
+                )
+        for step in range(depth):
+            for h in range(2):
+                arrived(h, far[h], (z + depth - step) % depth)
+        answer(far)
+        for step in range(depth):
+            for h in range(2):
+                arrived(h, across, (z + depth - step) % depth)
+        answer((across, across))
+        for step in range(1, depth + 1):
+            for h in range(2):
+                block = (z + step) % depth
+                send_back(
+                    h, parts.at[layer, h, across, block], first_in.at[layer, h, 1, block],
+                    depth + block, z * 4 + near[h],
+                )
+        for step in range(1, depth + 1):
+            for h in range(2):
+                block = (z + step) % depth
+                came_back(h, first_in.at[layer, h, 1, block], depth + block)
+                parts[layer, h, far[h], block] = (
+                    parts[layer, h, far[h], block].astype(jnp.float32)
+                    + first_in[layer, h, 1, block].astype(jnp.float32)
+                ).astype(jnp.bfloat16)
+                send_back(
+                    h, parts.at[layer, h, far[h], block], second_in.at[layer, h, block],
+                    2 * depth + block, z * 4 + far[h],
+                )
+        for step in range(1, depth + 1):
+            for h in range(2):
+                block = (z + step) % depth
+                came_back(h, first_in.at[layer, h, 0, block], block)
+                came_back(h, second_in.at[layer, h, block], 2 * depth + block)
+                total = (
+                    parts[layer, h, column, block].astype(jnp.float32)
+                    + first_in[layer, h, 0, block].astype(jnp.float32)
+                    + second_in[layer, h, block].astype(jnp.float32)
+                )
+                if step < depth:
+                    parts[layer, h, column, block] = total.astype(jnp.bfloat16)
+                    send_back(
+                        h, parts.at[layer, h, column, block], third_in.at[layer, h, z],
+                        3 * depth + z, block * 4 + column,
+                    )
+                    continue
+                for other in range(1, depth):
+                    source = (z + depth - other) % depth
+                    came_back(h, third_in.at[layer, h, source], 3 * depth + source)
+                    total = total + third_in[layer, h, source].astype(jnp.float32)
+                here = pl.ds(h * half_rows, half_rows)
+                rows[here, :] = (rows[here, :].astype(jnp.float32) + total).astype(jnp.bfloat16)
+        for _, copy in sends + backs:
+            copy.wait_send()
+        return carry
+
+    lax.fori_loop(0, layers, layer_body, 0)
+
+    final[...] = rows[...]
+    pooled = jnp.mean(rows[...].astype(jnp.float32).reshape(-1, SEQ, width), axis=1)
+    embedded = pooled * lax.rsqrt(jnp.sum(pooled * pooled, axis=1, keepdims=True) + EPSILON)
+    embedded = embedded.astype(jnp.bfloat16).astype(jnp.float32)
+    half_count, chunk = embedded.shape[0] // 2, embeds.shape[3]
+    per_row = width // chunk
+    for i in range(half_count * per_row):
+        j = half_count + i // per_row
+        first = i % per_row * chunk
+        embeds[core, me, pl.ds(i, 1), :] = embedded[j : j + 1, first : first + chunk]
+    slot = embeds.at[core, me]
+    copies = []
+    for step in range(1, experts):
+        copy = remote(
+            slot, slot, emb_send.at[step - 1], emb_recv.at[me], (core, (me + step) % experts)
+        )
+        copy.start()
+        copies.append(copy)
+    for step in range(1, experts):
+        source = (me + step) % experts
+        other = embeds.at[core, source]
+        remote(other, other, emb_send.at[0], emb_recv.at[source], (core, me)).wait_recv()
+    swap = remote(
+        embeds.at[core], embeds.at[core], pair_sem.at[0], pair_sem.at[1], (1 - core, me)
+    )
+    swap.start()
+    theirs = embeds.at[1 - core]
+    remote(theirs, theirs, pair_sem.at[0], pair_sem.at[1], (1 - core, me)).wait_recv()
+    swap.wait_send()
+    for copy in copies + swaps:
+        copy.wait_send()
+    passages[...] = embeds[...]
+
+
+def sections(
+    tokens, routing, norm_gain, router_weight, expert_gate_up, expert_down, pair_index, topic_ids
+):
+    layers, experts = routing.shape[0], router_weight.shape[2]
+    _, row_count, width = tokens.shape
+    depth, half_rows, ff = experts // 4, row_count // 2, expert_down.shape[2]
+    pooled_count = row_count // SEQ // 2
+    chunk = pooled_count * width // 8
+    guide = jnp.concatenate(
+        [
+            jnp.tile(router_weight[0].T, (LANES // experts, 1)),
+            jnp.broadcast_to(norm_gain, (16, width)),
+        ]
+    )
+    vmem, bf16 = pltpu.VMEM, jnp.bfloat16
+    dma = pltpu.SemaphoreType.DMA
+    block = (half_rows, width)
+    in_vmem, anywhere = pl.BlockSpec(memory_space=vmem), pl.BlockSpec(memory_space=pl.ANY)
+    final, passages = pl.pallas_call(
+        functools.partial(sections_kernel, (layers, experts, depth, row_count, width)),
+        out_shape=(
+            jax.ShapeDtypeStruct((row_count, width), bf16),
+            jax.ShapeDtypeStruct((2, experts, 8, chunk), jnp.float32),
+        ),
+        in_specs=[in_vmem, in_vmem, anywhere, anywhere, anywhere],
+        out_specs=(in_vmem, in_vmem),
+        scratch_shapes=[
+            vmem((row_count, width), bf16),
+            vmem((layers, LANES + 16, width), bf16),
+            vmem((layers, width, 2 * ff), bf16),
+            vmem((layers, ff, width), bf16),
+            vmem((layers, 2, 4, depth, half_rows, width + LANES), bf16),
+            vmem((layers, 2, 4, depth, *block), bf16),
+            vmem((layers, 2, 2, depth, *block), bf16),
+            vmem((layers, 2, depth, *block), bf16),
+            vmem((layers, 2, depth, *block), bf16),
+            vmem((2, experts, 8, chunk), jnp.float32),
+            dma((layers,)),
+            dma((layers,)),
+            dma((layers,)),
+            dma((3,)),
+            dma((layers, 2, experts - 1)),
+            dma((layers, 2, 4, depth)),
+            dma((layers, 2, experts - 1)),
+            dma((layers, 2, experts)),
+            dma((experts - 1,)),
+            dma((experts,)),
+            dma((2,)),
+        ],
+        compiler_params=pltpu.CompilerParams(
+            collective_id=0, has_side_effects=True, vmem_limit_bytes=56 * 1024 * 1024
+        ),
+    )(tokens, routing, guide, expert_gate_up, expert_down)
+    return final[None], contrastive(final, pair_index, topic_ids, passages.reshape(-1, width).astype(bf16))
+
+
 def solution(mesh):
     in_specs = (
         P(None, "expert", None),
@@ -100,4 +410,6 @@
         P(),
     )
     out_specs = (P("segment", "expert", None), P(("segment", "expert")))
-    return jax.shard_map(gathered, mesh=mesh, in_specs=in_specs, out_specs=out_specs, check_vma=False)
+    experts = mesh.shape["expert"]
+    fits = experts % 4 == 0 and experts * 2 <= 32 and mesh.shape["segment"] == 2
+    return jax.shard_map(sections if fits else gathered, mesh=mesh, in_specs=in_specs, out_specs=out_specs, check_vma=False)

time: 460 us -> 232 us (0.50)
  waiting for transfers between devices: 313 us -> 0 us
  Pallas kernels: 0 us -> 224 us
  blocking collectives: 89.6 us -> 0 us
  matrix products: 25.3 us -> 0.36 us
  between operations: 13.9 us -> 0.7 us
  starting transfers between devices: 8.46 us -> 0 us
  other arithmetic: 8.23 us -> 3.62 us
    pallas_call x0 -> x1, Pallas kernels: none -> 224 us  [sections(): pl.pallas_call(functools.partial(sections_kernel, (layers, experts, depth...]
    reduce_scatter x2 -> x0, waiting for transfers between devices: 189 us -> none  [gathered(): mixture = lax.psum_scatter(part, 'expert', scatter_dimension=0, tiled=True)]
    all_gather x2 -> x0, waiting for transfers between devices: 117 us -> none  [gathered(): everyone = lax.all_gather(normed, 'expert', axis=0, tiled=True)]
    all_gather x3 -> x0, blocking collectives: 78.4 us -> none  [the longest x1 69.4 us: contrastive(): lax.all_gather(embedded[half_count:], ('segment', 'expert'), axis=0, tile...]
    dot_general x6 -> x0, matrix products: 25 us -> none  [the longest x2 12.5 us: gathered(): jnp.dot(everyone, gate_ups[layer], preferred_element_type=jnp.float32)]
    all_to_all x1 -> x0, blocking collectives: 11.2 us -> none  [gathered(): lax.all_to_all(gates, 'expert', split_axis=1, concat_axis=0, tiled=True)]
    all_to_all x1 -> x0, starting transfers between devices: 7.73 us -> none  [gathered(): lax.all_to_all(gates, 'expert', split_axis=1, concat_axis=0, tiled=True)]
    all_to_all x1 -> x0, waiting for transfers between devices: 6.06 us -> none  [gathered(): lax.all_to_all(gates, 'expert', split_axis=1, concat_axis=0, tiled=True)]
  transfers between devices with their start and end apart: 7 -> 0, of which waited for: 5 -> 0; matrix products, arithmetic and copies ran while one was open for 2% -> 0% of each run, Pallas kernels for 0% -> 0%
where the time goes in v2:
time: 232 us
  Pallas kernels  224 us (97%)
  other arithmetic  3.62 us (2%)
  local copies, waits for them, and re-layouts  3.32 us (1%)
    pallas_call x1, Pallas kernels, sections(): pl.pallas_call(functools.partial(sections_kernel, (layers, experts, depth...  224 us

profile of v2, /device:TPU:1, one launch (start us, length us, event | category | flops | bytes accessed | tf_op | source)
XLA Modules:
  0.0 232.1 jit_solution(5361655062143577518)
XLA Ops:
  0.6 1.5 copy.11.routing
  2.1 0.7 reduce
  2.8 0.9 tile.4
  3.7 0.9 pad_maximum_fusion.guide
  4.6 0.0 copy-start.1
  4.6 0.0 copy-start.2
  4.6 224.1 %shard_map.95 = (bf16[64,2048]{1,0:T(8,128)(2,1)}, f32[2,16,8,512]{3,2,1,0:T(8,128)}) custom-call(bf16[2,64,2048]{2,1,0:T(8,128)(2,1)} %tokens.1, s32[2,2,64,8]{3,2,1,0:T(8,128)} %copy.11.routing, bf16[144,2048]{1,0:T(8,128)(2,1)} %pad_maximum_fusion.guide, bf16[1,1,2048,768]{3,2,1,0:T(8,128)(2,1)} %gate_up.1, bf16[1,1,384,2048]{3,2,1,0:T(8,128)(2,1)} %down.1), custom_call_target="tpu_custom_call" | custom-call | tf_op jit(solution)/shard_map/pallas_call | solution.py:363
  228.7 0.0 copy-start
  228.7 0.0 copy-done.1
  228.7 0.1 dynamic_slice.3
  228.8 0.0 copy-done.2
  228.8 0.2 select_reduce_fusion.1
  229.0 1.1 convert_element_type.11
  230.1 0.2 convert_element_type.12
  230.2 0.0 copy-done
  230.2 0.1 convert_reduce_fusion
  230.3 0.1 multiply_reduce_fusion
  230.5 0.4 fusion.2
  230.8 0.5 log_subtract_fusion
  231.4 0.7 copy.13
  (2 shorter events, 0.0 us)
Async XLA Ops:
  4.6 224.1 %copy-start.1 = (s32[64]{0:T(128)S(1)}, s32[64]{0:T(128)}, u32[]{:S(2)}) copy-start(s32[64]{0:T(128)} %param.14) | copy-start | bytes 772
  4.6 224.2 %copy-start.2 = (s32[64]{0:T(128)S(1)}, s32[64]{0:T(128)}, u32[]{:S(2)}) copy-start(s32[64]{0:T(128)} %param.15) | copy-start | bytes 772
  228.7 1.5 copy-start

commit v3 on v2

--- a/solution.py
+++ b/solution.py
@@ -111,6 +111,7 @@
     y, x = column // 2, column % 2
     beside_x, beside_y = y * 2 + 1 - x, (1 - y) * 2 + x
     across = (1 - y) * 2 + 1 - x
+    order = [z, z + 1 - 2 * (z % 2), (z + 2) % 4, 3 - z][:depth]
     near, far = (beside_y, beside_x), (beside_x, beside_y)
 
     barrier = pltpu.get_barrier_semaphore()
@@ -130,20 +131,26 @@
     weights = ((guide, guides, guide_sem), (gate_up.at[0, 0], ups, up_sem),
                (down.at[0, 0], downs, down_sem))
     swaps = []
-    for i, (src, dst, sem) in enumerate(weights):
+
+    def share(i):
+        src, dst, sem = weights[i]
         pltpu.make_async_copy(src, dst.at[core], sem.at[core]).start()
         swap = remote(src, dst.at[core], swap_sem.at[i], sem.at[core], (1 - core, me))
         swap.start()
         swaps.append(swap)
 
-    rows[...] = tokens[core]
-
     def landed(i, layer):
         src, dst, sem = weights[i]
         pltpu.make_async_copy(src, dst.at[layer], sem.at[layer]).wait()
 
+    share(0)
+    rows[...] = tokens[core]
+    for layer in range(layers):
+        landed(0, layer)
+    share(1)
+    share(2)
+
     def layer_body(layer, carry):
-        landed(0, layer)
         widened = rows[...].astype(jnp.float32)
         gain = guides[layer, pl.ds(LANES, 16), :][:1].astype(jnp.float32)
         normed = (
@@ -190,18 +197,21 @@
                 out_recv.at[layer, h, block_column, block_z], (core, me),
             ).wait_recv()
 
+        for block in order[1:]:
+            for h in range(2):
+                pass_on(h, column, z, block * 4 + column)
         for h in range(2):
             pass_on(h, column, z, z * 4 + near[h])
-        for step in range(1, depth):
-            for h in range(2):
-                pass_on(h, column, z, (z + step) % depth * 4 + column)
-        for step in range(1, depth):
-            for h in range(2):
-                arrived(h, column, (z + depth - step) % depth)
-                pass_on(h, column, (z + depth - step) % depth, z * 4 + near[h])
-        for step in range(depth):
-            for h in range(2):
-                pass_on(h, column, (z + depth - step) % depth, z * 4 + far[h])
+            pass_on(h, column, z, z * 4 + far[h])
+        for step in range(1, depth + 1):
+            for h in range(2):
+                if step < depth:
+                    arrived(h, column, order[step])
+                    pass_on(h, column, order[step], z * 4 + near[h])
+                    pass_on(h, column, order[step], z * 4 + far[h])
+            for h in range(2):
+                arrived(h, near[h], order[step - 1])
+                pass_on(h, near[h], order[step - 1], z * 4 + far[h])
         landed(1, layer)
         landed(2, layer)
 
@@ -239,37 +249,32 @@
             ).wait_recv()
 
         answer((column, column))
-        for step in range(depth):
-            for h in range(2):
-                block = (z + depth - step) % depth
-                arrived(h, near[h], block)
-                pass_on(h, near[h], block, z * 4 + far[h])
         answer(near)
         for step in range(depth):
             for h in range(2):
-                block = (z + step) % depth
+                block = order[step % depth]
                 send_back(
                     h, parts.at[layer, h, near[h], block], first_in.at[layer, h, 0, block],
                     block, z * 4 + near[h],
                 )
         for step in range(depth):
             for h in range(2):
-                arrived(h, far[h], (z + depth - step) % depth)
+                arrived(h, far[h], order[step])
         answer(far)
         for step in range(depth):
             for h in range(2):
-                arrived(h, across, (z + depth - step) % depth)
+                arrived(h, across, order[step])
         answer((across, across))
         for step in range(1, depth + 1):
             for h in range(2):
-                block = (z + step) % depth
+                block = order[step % depth]
                 send_back(
                     h, parts.at[layer, h, across, block], first_in.at[layer, h, 1, block],
                     depth + block, z * 4 + near[h],
                 )
         for step in range(1, depth + 1):
             for h in range(2):
-                block = (z + step) % depth
+                block = order[step % depth]
                 came_back(h, first_in.at[layer, h, 1, block], depth + block)
                 parts[layer, h, far[h], block] = (
                     parts[layer, h, far[h], block].astype(jnp.float32)
@@ -281,7 +286,7 @@
                 )
         for step in range(1, depth + 1):
             for h in range(2):
-                block = (z + step) % depth
+                block = order[step % depth]
                 came_back(h, first_in.at[layer, h, 0, block], block)
                 came_back(h, second_in.at[layer, h, block], 2 * depth + block)
                 total = (
@@ -297,7 +302,7 @@
                     )
                     continue
                 for other in range(1, depth):
-                    source = (z + depth - other) % depth
+                    source = order[other]
                     came_back(h, third_in.at[layer, h, source], 3 * depth + source)
                     total = total + third_in[layer, h, source].astype(jnp.float32)
                 here = pl.ds(h * half_rows, half_rows)
@@ -411,5 +416,5 @@
     )
     out_specs = (P("segment", "expert", None), P(("segment", "expert")))
     experts = mesh.shape["expert"]
-    fits = experts % 4 == 0 and experts * 2 <= 32 and mesh.shape["segment"] == 2
+    fits = experts in (4, 8, 16) and mesh.shape["segment"] == 2
     return jax.shard_map(sections if fits else gathered, mesh=mesh, in_specs=in_specs, out_specs=out_specs, check_vma=False)

time: 232 us -> 209 us (0.901)
  Pallas kernels: 224 us -> 201 us
    pallas_call x1, Pallas kernels: 224 us -> 201 us  [sections(): pl.pallas_call(functools.partial(sections_kernel, (layers, experts, depth...]
where the time goes in v3:
time: 209 us
  Pallas kernels  201 us (96%)
  other arithmetic  3.62 us (2%)
  local copies, waits for them, and re-layouts  3.32 us (2%)
    pallas_call x1, Pallas kernels, sections(): pl.pallas_call(functools.partial(sections_kernel, (layers, experts, depth...  201 us

profile of v3, /device:TPU:1, one launch (start us, length us, event | category | flops | bytes accessed | tf_op | source)
XLA Modules:
  0.0 208.5 jit_solution(15889209412888102006)
XLA Ops:
  0.6 1.5 copy.11.routing
  2.1 0.7 reduce
  2.8 0.9 tile.4
  3.7 0.9 pad_maximum_fusion.guide
  4.6 0.0 copy-start.1
  4.6 0.0 copy-start.2
  4.6 200.5 %shard_map.95 = (bf16[64,2048]{1,0:T(8,128)(2,1)}, f32[2,16,8,512]{3,2,1,0:T(8,128)}) custom-call(bf16[2,64,2048]{2,1,0:T(8,128)(2,1)} %tokens.1, s32[2,2,64,8]{3,2,1,0:T(8,128)} %copy.11.routing, bf16[144,2048]{1,0:T(8,128)(2,1)} %pad_maximum_fusion.guide, bf16[1,1,2048,768]{3,2,1,0:T(8,128)(2,1)} %gate_up.1, bf16[1,1,384,2048]{3,2,1,0:T(8,128)(2,1)} %down.1), custom_call_target="tpu_custom_call" | custom-call | tf_op jit(solution)/shard_map/pallas_call | solution.py:368
  205.2 0.0 copy-start
  205.2 0.0 copy-done.1
  205.2 0.1 dynamic_slice.3
  205.3 0.0 copy-done.2
  205.3 0.2 select_reduce_fusion.1
  205.4 1.1 convert_element_type.11
  206.5 0.2 convert_element_type.12
  206.7 0.0 copy-done
  206.7 0.1 convert_reduce_fusion
  206.8 0.1 multiply_reduce_fusion
  206.9 0.4 fusion.2
  207.3 0.5 log_subtract_fusion
  207.8 0.7 copy.13
  (2 shorter events, 0.0 us)
Async XLA Ops:
  4.6 200.6 %copy-start.1 = (s32[64]{0:T(128)S(1)}, s32[64]{0:T(128)}, u32[]{:S(2)}) copy-start(s32[64]{0:T(128)} %param.14) | copy-start | bytes 772
  4.6 200.7 %copy-start.2 = (s32[64]{0:T(128)S(1)}, s32[64]{0:T(128)}, u32[]{:S(2)}) copy-start(s32[64]{0:T(128)} %param.15) | copy-start | bytes 772
  205.2 1.5 copy-start

commit v4 on v3

--- a/solution.py
+++ b/solution.py
@@ -250,9 +250,8 @@
 
         answer((column, column))
         answer(near)
-        for step in range(depth):
-            for h in range(2):
-                block = order[step % depth]
+        for block in order[::-1]:
+            for h in range(2):
                 send_back(
                     h, parts.at[layer, h, near[h], block], first_in.at[layer, h, 0, block],
                     block, z * 4 + near[h],
@@ -265,16 +264,17 @@
             for h in range(2):
                 arrived(h, across, order[step])
         answer((across, across))
-        for step in range(1, depth + 1):
-            for h in range(2):
-                block = order[step % depth]
+        for block in order[::-1]:
+            for h in range(2):
                 send_back(
                     h, parts.at[layer, h, across, block], first_in.at[layer, h, 1, block],
                     depth + block, z * 4 + near[h],
                 )
-        for step in range(1, depth + 1):
-            for h in range(2):
-                block = order[step % depth]
+        for step in range(depth + 1):
+            for h in range(2):
+                if step == depth:
+                    continue
+                block = order[depth - 1 - step]
                 came_back(h, first_in.at[layer, h, 1, block], depth + block)
                 parts[layer, h, far[h], block] = (
                     parts[layer, h, far[h], block].astype(jnp.float32)
@@ -284,9 +284,10 @@
                     h, parts.at[layer, h, far[h], block], second_in.at[layer, h, block],
                     2 * depth + block, z * 4 + far[h],
                 )
-        for step in range(1, depth + 1):
-            for h in range(2):
-                block = order[step % depth]
+            for h in range(2):
+                if step == 0:
+                    continue
+                block = order[depth - step]
                 came_back(h, first_in.at[layer, h, 0, block], block)
                 came_back(h, second_in.at[layer, h, block], 2 * depth + block)
                 total = (

time: 209 us -> 203 us (0.971)
  Pallas kernels: 201 us -> 194 us
    pallas_call x1, Pallas kernels: 201 us -> 194 us  [sections(): pl.pallas_call(functools.partial(sections_kernel, (layers, experts, depth...]
where the time goes in v4:
time: 203 us; the launch traced here: 202 us
  Pallas kernels  194 us (96%)
  other arithmetic  3.62 us (2%)
  local copies, waits for them, and re-layouts  3.32 us (2%)
    pallas_call x1, Pallas kernels, sections(): pl.pallas_call(functools.partial(sections_kernel, (layers, experts, depth...  194 us

profile of v4, /device:TPU:1, one launch (start us, length us, event | category | flops | bytes accessed | tf_op | source)
XLA Modules:
  0.0 202.4 jit_solution(2508481549510378188)
XLA Ops:
  0.6 1.5 copy.11.routing
  2.1 0.7 reduce
  2.8 0.9 tile.4
  3.7 0.9 pad_maximum_fusion.guide
  4.6 0.0 copy-start.1
  4.6 0.0 copy-start.2
  4.6 194.4 %shard_map.95 = (bf16[64,2048]{1,0:T(8,128)(2,1)}, f32[2,16,8,512]{3,2,1,0:T(8,128)}) custom-call(bf16[2,64,2048]{2,1,0:T(8,128)(2,1)} %tokens.1, s32[2,2,64,8]{3,2,1,0:T(8,128)} %copy.11.routing, bf16[144,2048]{1,0:T(8,128)(2,1)} %pad_maximum_fusion.guide, bf16[1,1,2048,768]{3,2,1,0:T(8,128)(2,1)} %gate_up.1, bf16[1,1,384,2048]{3,2,1,0:T(8,128)(2,1)} %down.1), custom_call_target="tpu_custom_call" | custom-call | tf_op jit(solution)/shard_map/pallas_call | solution.py:369
  199.0 0.0 copy-start
  199.0 0.0 copy-done.1
  199.0 0.1 dynamic_slice.3
  199.1 0.0 copy-done.2
  199.1 0.2 select_reduce_fusion.1
  199.3 1.1 convert_element_type.11
  200.4 0.2 convert_element_type.12
  200.5 0.0 copy-done
  200.5 0.1 convert_reduce_fusion
  200.6 0.1 multiply_reduce_fusion
  200.8 0.4 fusion.2
  201.1 0.5 log_subtract_fusion
  201.7 0.7 copy.13
  (2 shorter events, 0.0 us)
Async XLA Ops:
  4.6 194.4 %copy-start.1 = (s32[64]{0:T(128)S(1)}, s32[64]{0:T(128)}, u32[]{:S(2)}) copy-start(s32[64]{0:T(128)} %param.14) | copy-start | bytes 772
  4.6 194.5 %copy-start.2 = (s32[64]{0:T(128)S(1)}, s32[64]{0:T(128)}, u32[]{:S(2)}) copy-start(s32[64]{0:T(128)} %param.15) | copy-start | bytes 772
  199.0 1.5 copy-start
